TPU v7x, 512 devices: a whole 4x8x8 slice. The times are simulated.
512 devices in a mesh: user: 16 (over z, core), ctx: 8 (over y), head: 4 (over x).
Axes of the slice: x: 4, y: 8, z: 8, core: 2. Of those that a mesh axis runs over, the one named last changes fastest.
Arguments:
- catalog: bfloat16 [8192, 1024], P('user'), may hold values from -6 to 6
- cand_owner: int32 [16, 2048, 1], P('user', 'ctx'), may hold values from 0 to 15; in each aligned block of 256 rows (0 to 255, 256 to 511, ..., all dimensions but the last counted through in order) at most 32 rows name the same one
- cand_row: int32 [16, 2048], P('user', 'ctx'), may hold values from 0 to 511
- hist_len: int32 [16], P('user'), may hold values from 3072 to 12288, as said below
- proj_weight: bfloat16 [1024, 2, 1024], P(None, None, 'head'), may hold values from -0.1875 to 0.1875
- keys: bfloat16 [16, 12288, 1024], P('user', 'ctx', 'head'), may hold values from -6 to 6
- values: bfloat16 [16, 12288, 1024], P('user', 'ctx', 'head'), may hold values from -1280 to 1280
- out_weight: bfloat16 [1024, 1024], P('head'), may hold values from -0.1875 to 0.1875
Outputs:
- ranked: bfloat16 [16, 2048, 1024], P('user', 'ctx', 'head')
Inputs may be any that keep to these rules, and one draw needn't show every extreme that they name: `cand_owner`: within each aligned block of 256 shortlisted items of one user (one ctx index), at most 32 are owned by the same catalog shard. `hist_len`: at least one user has all 12288 events.
All inputs are finite; a program needn't handle non-finite values.
Results may differ from a plain program's by a relative error of at most 0.0071.
Values may be sent and summed in bfloat16 or wider, within the bound.
A program may use at most 64 MiB of HBM per device.

v0:
```python
import jax
import jax.numpy as jnp
from jax import lax
from jax.sharding import PartitionSpec as P

HEAD = 128


def joined_along(pieces, dim):
    dims = list(pieces.shape[1:])
    dims[dim] *= pieces.shape[0]
    return jnp.moveaxis(pieces, 0, dim).reshape(dims)


def copy_for_each(value, axis):
    size = lax.axis_size(axis)
    return lax.all_to_all(
        jnp.broadcast_to(value[None], (size, *value.shape)), axis, 0, 0, tiled=True
    )


def gather_directly(value, axis, dim):
    return joined_along(copy_for_each(value, axis), dim)


def cut_along(value, dim, size):
    before, after = (value.shape[:dim], value.shape[dim + 1 :])
    return jnp.moveaxis(value.reshape(*before, size, -1, *after), dim, 0)


def sum_at_owner(value, axis, dim):
    pieces = cut_along(value, dim, lax.axis_size(axis))
    arrived = lax.all_to_all(pieces, axis, split_axis=0, concat_axis=0, tiled=True)
    return arrived.sum(axis=0)


def attend_block(query_rows, key_rows, value_rows, offset, length):
    row_total = query_rows.shape[0]
    key_total = key_rows.shape[0]
    head_count = query_rows.shape[1] // HEAD
    query_heads = query_rows.reshape(row_total, head_count, HEAD)
    key_heads = key_rows.reshape(key_total, head_count, HEAD)
    value_heads = value_rows.reshape(key_total, head_count, HEAD)
    scores = jnp.einsum(
        "rhc,nhc->rhn", query_heads, key_heads, preferred_element_type=jnp.float32
    ) * HEAD ** (-0.5)
    places = offset + jnp.arange(key_total, dtype=jnp.int32)
    weights = jnp.where(
        places[None, None, :] < length, jax.nn.silu(scores) / length.astype(jnp.float32), 0.0
    ).astype(jnp.bfloat16)
    mixed_rows = jnp.einsum(
        "rhn,nhc->rhc", weights, value_heads, preferred_element_type=jnp.float32
    )
    return mixed_rows.reshape(row_total, head_count * HEAD)


def per_device(catalog, cand_owner, cand_row, hist_len, proj_weight, keys, values, out_weight):
    user_count = lax.axis_size("user")
    owners = cand_owner[0, :, 0]
    wanted = cand_row[0]
    cand_count = wanted.shape[0]
    slot_count = 2 * cand_count // user_count
    model_width = catalog.shape[1]
    col_share = proj_weight.shape[2]
    owner_hot = (owners[:, None] == jnp.arange(user_count, dtype=jnp.int32)[None, :]).astype(
        jnp.int32
    )
    rank_in = jnp.sum(jnp.cumsum(owner_hot, axis=0) * owner_hot, axis=1) - 1
    places = owners * slot_count + rank_in
    request = (
        jnp.zeros((user_count * slot_count,), jnp.int32)
        .at[places]
        .set(wanted)
        .reshape(user_count, slot_count)
    )
    weight_flat = proj_weight.reshape(model_width, 2 * col_share)
    asked_ids = lax.all_to_all(request, "user", split_axis=0, concat_axis=0, tiled=True)
    picked = jax.nn.silu(
        jnp.dot(
            jnp.take(catalog, asked_ids.reshape(-1), axis=0),
            weight_flat,
            preferred_element_type=jnp.float32,
        )
    ).astype(jnp.bfloat16)
    served = picked.reshape(asked_ids.shape[0], asked_ids.shape[1], 2 * col_share)
    returned = lax.all_to_all(served, "user", split_axis=0, concat_axis=0, tiled=True)
    own_rows = jnp.take(returned.reshape(user_count * slot_count, 2 * col_share), places, axis=0)
    queries = own_rows[:, :col_share]
    gates = own_rows[:, col_share:]
    length = hist_len[0]
    key_rows = keys[0]
    value_rows = values[0]
    all_queries = gather_directly(queries, "ctx", 0)
    offset = lax.axis_index("ctx") * key_rows.shape[0]
    attended = lax.psum_scatter(
        attend_block(all_queries, key_rows, value_rows, offset, length),
        "ctx",
        scatter_dimension=0,
        tiled=True,
    )
    gated_rows = (attended * gates.astype(jnp.float32)).astype(jnp.bfloat16)
    partials = jnp.dot(gated_rows, out_weight, preferred_element_type=jnp.float32)
    ranked = sum_at_owner(partials, "head", 1).astype(jnp.bfloat16)
    return ranked.reshape(1, cand_count, col_share)


def solution(mesh):
    return jax.shard_map(
        per_device,
        mesh=mesh,
        in_specs=(
            P("user", None),
            P("user", "ctx", None),
            P("user", "ctx"),
            P("user"),
            P(None, None, "head"),
            P("user", "ctx", "head"),
            P("user", "ctx", "head"),
            P("head", None),
        ),
        out_specs=P("user", "ctx", "head"),
        check_vma=False,
    )
```

profile of v0, /device:TPU:8, one launch (start us, length us, event | category | flops | bytes accessed | tf_op | source)
XLA Modules:
  0.0 171.5 jit_solution(12336367109615690039)
XLA Ops:
  6.5 0.8 fusion.19
  7.3 0.6 reduce-window.6
  7.9 0.2 slice_reduce_fusion
  8.1 0.8 fusion.18
  8.9 0.7 compare_select_fusion.1
  9.6 1.6 scatter_custom_fusion
  11.1 0.7 all_to_all.15
  11.8 10.4 %all-to-all-start = ((s32[16,1,32]{2,1,0:T(1,128)}), s32[16,1,32]{2,1,0:T(1,128)S(1)}, u32[]{:S(2)}, u32[]{:S(2)}) async-start(s32[16,1,32]{2,1,0:T(1,128)} %all_to_all.15), calls=%async_computation | async-start | bytes 16384 | tf_op jit(solution)/shard_map/all_to_all | solution.py:77
  22.2 1.5 copy.30
  23.7 6.0 %all-to-all-done = s32[16,1,32]{2,1,0:T(1,128)S(1)} async-done(((s32[16,1,32]{2,1,0:T(1,128)}), s32[16,1,32]{2,1,0:T(1,128)S(1)}, u32[]{:S(2)}, u32[]{:S(2)}) %all-to-all-start) | async-done | bytes 2080 | tf_op jit(solution)/shard_map/all_to_all | solution.py:77
  29.8 0.5 broadcast.125
  30.3 0.7 reduce.7
  31.1 2.1 %gather_fusion = bf16[512,1024]{1,0:T(8,128)(2,1)S(1)} fusion(bf16[512,1024]{1,0:T(8,128)(2,1)S(1)} %copy-done, s32[1024]{0:T(1024)S(1)} %pad_clamp_fusion.1), kind=kCustom, calls=%fused_computation | custom fusion | bytes 2099200 | tf_op jit(solution)/shard_map/jit(_take)/gather | solution.py:80
  33.2 1.7 multiply_convert_fusion
  34.9 3.6 %all-to-all-start.1 = ((bf16[16,32,512]{2,1,0:T(8,128)(2,1)}), bf16[16,32,512]{2,1,0:T(8,128)(2,1)S(1)}, u32[]{:S(2)}, u32[]{:S(2)}) async-start(bf16[16,32,512]{2,1,0:T(8,128)(2,1)} %bitcast.80), calls=%async_computation.1 | async-start | bytes 1048576 | tf_op jit(solution)/shard_map/all_to_all | solution.py:86
  38.5 15.9 %all-to-all-done.1 = bf16[16,32,512]{2,1,0:T(8,128)(2,1)S(1)} async-done(((bf16[16,32,512]{2,1,0:T(8,128)(2,1)}), bf16[16,32,512]{2,1,0:T(8,128)(2,1)S(1)}, u32[]{:S(2)}, u32[]{:S(2)}) %all-to-all-start.1) | async-done | bytes 524320 | tf_op jit(solution)/shard_map/all_to_all | solution.py:86
  54.4 1.2 gather_fusion.1
  55.5 0.1 broadcast_select_fusion
  55.7 0.1 copy.19
  55.8 1.1 broadcast_in_dim.53
  56.8 7.5 %all-to-all-start.2 = ((bf16[8,256,256]{1,2,0:T(8,128)(2,1)}), bf16[8,256,256]{1,2,0:T(8,128)(2,1)S(1)}, u32[]{:S(2)}, u32[]{:S(2)}) async-start(bf16[8,256,256]{1,2,0:T(8,128)(2,1)} %broadcast_in_dim.53), calls=%async_computation.2 | async-start | bytes 2097152 | tf_op jit(solution)/shard_map/all_to_all | solution.py:17
  65.1 1.1 reshape_squeeze.6
  66.1 2.3 %copy.27 = bf16[1,1536,256]{1,2,0:T(8,128)(2,1)} copy(bf16[1,1536,256]{2,1,0:T(8,128)(2,1)} %param.14) | data formatting | bytes 1572864 | tf_op jit(solution)/shard_map/reshape;squeeze | solution.py:43
  68.5 24.2 %all-to-all-done.2 = bf16[8,256,256]{1,2,0:T(8,128)(2,1)S(1)} async-done(((bf16[8,256,256]{1,2,0:T(8,128)(2,1)}), bf16[8,256,256]{1,2,0:T(8,128)(2,1)S(1)}, u32[]{:S(2)}, u32[]{:S(2)}) %all-to-all-start.2) | async-done | bytes 1048608 | tf_op jit(solution)/shard_map/all_to_all | solution.py:17
  92.7 0.6 copy.20
  93.3 1.5 reshape_reshape.3
  94.8 13.1 %fusion.6 = f32[2,2048,128]{1,2,0:T(8,128)S(1)} fusion(bf16[1536,2,128]{0,2,1:T(8,128)(2,1)} %bitcast.79, bf16[2048,2,128]{0,2,1:T(8,128)(2,1)} %reshape_reshape.3, f32[]{:T(128)S(6)} %convert_element_type.35, pred[1536]{0:T(1024)(128)(4,1)S(1)} %add_compare_fusion, bf16[1536,2,128]{2,1,0:T(2,128)(2,1)} %reshape_squeeze.6), kind=kOutput, calls=%fused_computation.11 | convolution fusion | flops 3271557120 | bytes 4720132 | tf_op jit(solution)/shard_map/rhn,nhc->rhc/dot_general | solution.py:51
  107.9 1.9 %copy.24 = f32[2048,256]{1,0:T(8,128)} copy(f32[2048,256]{0,1:T(8,128)S(1)} %bitcast.76) | data formatting | bytes 4194304 | tf_op jit(solution)/shard_map/reshape | solution.py:54
  109.8 37.8 %reduce-scatter.2.cloned.1.call-done = f32[256,256]{1,0:T(8,128)} async-done(((f32[2048,256]{1,0:T(8,128)}), f32[256,256]{1,0:T(8,128)}) %reduce-scatter.2.cloned.1.call-update) | async-done | bytes 262160 | tf_op jit(solution)/shard_map/reduce_scatter | solution.py:95
  147.6 1.3 fusion.15
  149.0 14.9 %all_to_all.24 = f32[4,256,256]{2,1,0:T(8,128)S(1)} all-to-all(f32[4,256,256]{2,1,0:T(8,128)S(1)} %bitcast.74), channel_id=1, replica_groups=mesh['user'=16,'ctx'=8,'head'=4] {'head'}, dimensions={0} | all-to-all | bytes 2097152 | tf_op jit(solution)/shard_map/all_to_all | solution.py:33
  163.9 0.7 reduce_sum.19
  (23 shorter events, 0.4 us)
Async XLA Ops:
  6.5 24.6 %copy-start = (bf16[512,1024]{1,0:T(8,128)(2,1)S(1)}, bf16[512,1024]{1,0:T(8,128)(2,1)}, u32[]{:S(2)}) copy-start(bf16[512,1024]{1,0:T(8,128)(2,1)} %param.8) | copy-start | bytes 3145732
  11.8 17.9 %all-to-all-start = ((s32[16,1,32]{2,1,0:T(1,128)}), s32[16,1,32]{2,1,0:T(1,128)S(1)}, u32[]{:S(2)}, u32[]{:S(2)}) async-start(s32[16,1,32]{2,1,0:T(1,128)} %all_to_all.15), calls=%async_computation | async-start | bytes 16384 | tf_op jit(solution)/shard_map/all_to_all | solution.py:77
  33.2 5.3 %copy-start.3 = (s32[1,256,1]{1,2,0:T(1,128)S(1)}, s32[1,256,1]{1,2,0:T(1,128)}, u32[]{:S(2)}) copy-start(s32[1,256,1]{1,2,0:T(1,128)} %param.9) | copy-start | bytes 3076
  34.9 19.5 %all-to-all-start.1 = ((bf16[16,32,512]{2,1,0:T(8,128)(2,1)}), bf16[16,32,512]{2,1,0:T(8,128)(2,1)S(1)}, u32[]{:S(2)}, u32[]{:S(2)}) async-start(bf16[16,32,512]{2,1,0:T(8,128)(2,1)} %bitcast.80), calls=%async_computation.1 | async-start | bytes 1048576 | tf_op jit(solution)/shard_map/all_to_all | solution.py:86
  55.5 9.5 %copy-start.1 = (bf16[1,1536,256]{2,1,0:T(8,128)(2,1)S(1)}, bf16[1,1536,256]{2,1,0:T(8,128)(2,1)}, u32[]{:S(2)}) copy-start(bf16[1,1536,256]{2,1,0:T(8,128)(2,1)} %param.13) | copy-start | bytes 2359300
  56.8 35.8 %all-to-all-start.2 = ((bf16[8,256,256]{1,2,0:T(8,128)(2,1)}), bf16[8,256,256]{1,2,0:T(8,128)(2,1)S(1)}, u32[]{:S(2)}, u32[]{:S(2)}) async-start(bf16[8,256,256]{1,2,0:T(8,128)(2,1)} %broadcast_in_dim.53), calls=%async_computation.2 | async-start | bytes 2097152 | tf_op jit(solution)/shard_map/all_to_all | solution.py:17
  64.4 83.3 %reduce-scatter.2.cloned.1.call-start = ((), (), s32[]{:S(2)}) async-start(), calls=%async_computation.5 | async-start | bytes 2359296 | tf_op jit(solution)/shard_map/reduce_scatter | solution.py:95
  109.8 37.9 %copy-start.2 = (bf16[256,1024]{1,0:T(8,128)(2,1)S(1)}, bf16[256,1024]{1,0:T(8,128)(2,1)}, u32[]{:S(2)}) copy-start(bf16[256,1024]{1,0:T(8,128)(2,1)} %param.15) | copy-start | bytes 1572868
Sparse Core Ops, SparseCore 0:
  109.9 37.6 reduce-scatter.1
where the time goes:
time: 172 us
  waiting for transfers between devices  84 us (49%)
  starting transfers between devices  21.5 us (12%)
  local copies, waits for them, and re-layouts  16.4 us (10%)
  matrix products  16.1 us (9%)
  blocking collectives  14.9 us (9%)
  between operations  14.2 us (8%)
  other arithmetic  4.4 us (3%)
    reduce_scatter x1, waiting for transfers between devices, per_device(): lax.psum_scatter(attend_block(all_queries, key_rows, value_rows, offset,...  37.8 us
    all_to_all x1, waiting for transfers between devices, copy_for_each(): lax.all_to_all(jnp.broadcast_to(value[None], (size, *value.shape)), axis,...  24.2 us
    all_to_all x1, waiting for transfers between devices, per_device(): lax.all_to_all(served, 'user', split_axis=0, concat_axis=0, tiled=True)  15.9 us
    all_to_all x1, blocking collectives, sum_at_owner(): lax.all_to_all(pieces, axis, split_axis=0, concat_axis=0, tiled=True)  14.9 us
    dot_general x1, matrix products, attend_block(): jnp.einsum('rhn,nhc->rhc', weights, value_heads, preferred_element_type=j...  13.1 us
    all_to_all x1, starting transfers between devices, per_device(): lax.all_to_all(request, 'user', split_axis=0, concat_axis=0, tiled=True)  10.4 us
    all_to_all x1, starting transfers between devices, copy_for_each(): lax.all_to_all(jnp.broadcast_to(value[None], (size, *value.shape)), axis,...  7.55 us
    all_to_all x1, waiting for transfers between devices, per_device(): lax.all_to_all(request, 'user', split_axis=0, concat_axis=0, tiled=True)  6.04 us
  transfers between devices with their start and end apart: 4, of which 4 were waited for; matrix products, arithmetic and copies ran while one was open for 3% of the time, Pallas kernels for 0%

commit v1 on v0

v1 whole, which is shorter than its diff:
```python
import functools

import jax
import jax.numpy as jnp
from jax import lax
from jax.experimental import pallas as pl
from jax.experimental.pallas import tpu as pltpu
from jax.sharding import PartitionSpec as P

HEAD = 128
MESH = pl.DeviceIdType.MESH
BF = jnp.bfloat16
F32 = jnp.float32
SLOTS = 32
KEY_STEP = 512


def send(src, dst, ssem, rsem, axis, index):
    return pltpu.make_async_remote_copy(
        src_ref=src, dst_ref=dst, send_sem=ssem, recv_sem=rsem,
        device_id={axis: index}, device_id_type=MESH,
    )


def column(row, lanes):
    tall = jnp.broadcast_to(row, (128, row.shape[1])).T
    return jnp.concatenate([tall] * (lanes // 128), axis=1)


def silu(v):
    return v / (1.0 + jnp.exp(-v))


def dot(a, b):
    return jnp.dot(a, b, preferred_element_type=F32)


def dot_t(a, b):
    return lax.dot_general(a, b, (((1,), (1,)), ((), ())), preferred_element_type=F32)


def kernel(
    n_user, n_ctx, n_head,
    cat_hbm, owner_ref, row_ref, len_ref, w_hbm, key_hbm, val_hbm, wout_hbm,
    out_ref,
    cat_v, w_v, key_v, val_v, wout_v,
    req_out, req_in, tab_q, tab_g, hot_v, unhot_v, sq, sg, rq, rg,
    q_all, acc, po, pin_l, pin_r, gate_v, g_all, wx,
    load_sem, req_ss, req_rs, sq_ss, sq_rs, sg_ss, sg_rs,
    ag_ss, ag_rs, rs_ss, rs_rs, wx_ss, wx_rs, xg_ss, xg_rs,
):
    u = lax.axis_index("user")
    c = lax.axis_index("ctx")
    h = lax.axis_index("head")
    right, left = lax.rem(c + 1, n_ctx), lax.rem(c + n_ctx - 1, n_ctx)
    cand = owner_ref.shape[1]
    half = cand // 2
    hist = key_v.shape[0]
    width = key_v.shape[1]
    slot_total = n_user * SLOTS

    loads = [
        pltpu.make_async_copy(a, b, load_sem.at[i])
        for i, (a, b) in enumerate(
            ((cat_hbm, cat_v), (w_hbm, w_v), (wout_hbm, wout_v), (key_hbm, key_v), (val_hbm, val_v))
        )
    ]
    for copy in loads:
        copy.start()

    barrier = pltpu.get_barrier_semaphore()

    def greet(d, _):
        pl.semaphore_signal(barrier, inc=1, device_id={"user": lax.rem(u + d, n_user)}, device_id_type=MESH)
        return 0

    lax.fori_loop(1, n_user, greet, 0)
    for other in (left, right):
        pl.semaphore_signal(barrier, inc=1, device_id={"ctx": other}, device_id_type=MESH)
    for k in range(1, n_head):
        pl.semaphore_signal(barrier, inc=1, device_id={"head": lax.rem(h + k, n_head)}, device_id_type=MESH)

    owner = owner_ref[...].astype(F32)
    owner_col = column(owner, cand)
    first = lax.broadcasted_iota(jnp.int32, (cand, cand), 0)
    second = lax.broadcasted_iota(jnp.int32, (cand, cand), 1)
    before = jnp.where((owner_col == owner) & (first < second), 1.0, 0.0)
    rank = jnp.sum(before, axis=0, keepdims=True)
    place_col = column(owner * SLOTS + rank, slot_total)
    slot_lane = lax.broadcasted_iota(jnp.int32, (cand, slot_total), 1).astype(F32)
    unhot_v[...] = jnp.where(place_col == slot_lane, 1.0, 0.0).astype(BF)
    rank_col = place_col[:, :128] - owner_col[:, :128] * SLOTS
    shift = (lax.rem(u, 4) * SLOTS).astype(F32)
    rank_hot = jnp.where(rank_col + shift == slot_lane[:, :128], 1.0, 0.0).astype(BF)
    wanted = row_ref[...]
    shard = lax.broadcasted_iota(jnp.int32, (n_user, cand), 0)
    mine = owner_ref[...] == shard
    high = jnp.where(mine, lax.shift_right_logical(wanted, 4).astype(F32), 0.0)
    low = jnp.where(mine, (wanted & 15).astype(F32), 0.0)
    asked = dot(jnp.concatenate([high, low], axis=0).astype(BF), rank_hot)
    asked = (asked[:n_user] * 16.0 + asked[n_user:]).astype(jnp.int32)
    for s in range(n_user):
        req_out[s] = asked[s:s + 1]

    pl.semaphore_wait(barrier, n_user - 1 + 2 + n_head - 1)

    def exchange(src, dst, ssem, rsem):
        def start(d, _):
            to = lax.rem(u + d, n_user)
            send(src.at[to], dst.at[u], ssem.at[d], rsem.at[d], "user", to).start()
            return 0

        lax.fori_loop(1, n_user, start, 0)
        dst[u] = src[u]

    def arrived(src, dst, ssem, rsem):
        def wait(d, _):
            origin = lax.rem(u + n_user - d, n_user)
            send(src.at[0], dst.at[origin], ssem.at[d], rsem.at[d], "user", lax.rem(u + d, n_user)).wait_recv()
            return 0

        lax.fori_loop(1, n_user, wait, 0)

    def drained(src, dst, ssem, rsem):
        def wait(d, _):
            to = lax.rem(u + d, n_user)
            send(src.at[to], dst.at[u], ssem.at[d], rsem.at[d], "user", to).wait_send()
            return 0

        lax.fori_loop(1, n_user, wait, 0)

    exchange(req_out, req_in, req_ss, req_rs)

    loads[0].wait()
    loads[1].wait()
    tab_q[...] = silu(dot(cat_v[...], w_v[0])).astype(BF)
    tab_g[...] = silu(dot(cat_v[...], w_v[1])).astype(BF)

    loads[2].wait()

    def wx_copy(k):
        to = lax.rem(h + k, n_head)
        cols = pl.ds(pl.multiple_of(to * width, width), width)
        return send(wout_v.at[:, cols], wx.at[k], wx_ss.at[k], wx_rs.at[k], "head", to)

    for k in range(1, n_head):
        wx_copy(k).start()
    wx[0] = wout_v[:, pl.ds(pl.multiple_of(h * width, width), width)]

    arrived(req_out, req_in, req_ss, req_rs)
    row_lane = lax.broadcasted_iota(jnp.int32, (128, cat_v.shape[0]), 1).astype(F32)
    for g in range(n_user // 4):
        ids = req_in[4 * g] + req_in[4 * g + 1] + req_in[4 * g + 2] + req_in[4 * g + 3]
        hot = jnp.where(column(ids.astype(F32), cat_v.shape[0]) == row_lane, 1.0, 0.0)
        hot_v[128 * g:128 * (g + 1)] = hot.astype(BF)
    sq[...] = dot(hot_v[...], tab_q[...]).astype(BF).reshape(sq.shape)
    exchange(sq, rq, sq_ss, sq_rs)
    sg[...] = dot(hot_v[...], tab_g[...]).astype(BF).reshape(sg.shape)
    exchange(sg, rg, sg_ss, sg_rs)

    loads[3].wait()
    loads[4].wait()
    length = len_ref[...]
    place = lax.broadcasted_iota(jnp.int32, (hist, width), 0) + c * hist
    val_v[...] = jnp.where(place < length, val_v[...].astype(F32), 0.0).astype(BF)
    scale = HEAD ** -0.5
    arg_scale = 0.5 * scale
    out_scale = jnp.broadcast_to((0.5 * scale) / length.astype(F32), (1, KEY_STEP))

    arrived(sq, rq, sq_ss, sq_rs)
    q_all[0] = dot(unhot_v[...], rq[...].reshape(slot_total, width)).astype(BF)

    def part(ref, block, ch):
        return ref.at[block, pl.ds(pl.multiple_of(ch * half, half), half)]

    def to_right(src_block, dst_block, ch, number):
        return send(part(q_all, src_block, ch), part(q_all, dst_block, ch),
                    ag_ss.at[0, number], ag_rs.at[0, number], "ctx", right)

    def to_left(src_block, dst_block, ch, number):
        return send(part(q_all, src_block, ch), part(q_all, dst_block, ch),
                    ag_ss.at[1, number], ag_rs.at[1, number], "ctx", left)

    for ch in (0, 1):
        to_right(0, 1, ch, ch + 1).start()
        to_left(0, n_ctx - 1, ch, ch + 1).start()

    def attend(block_a, ch_a, block_b, ch_b):
        queries = jnp.concatenate([part(q_all, block_a, ch_a)[...], part(q_all, block_b, ch_b)[...]], axis=0)
        totals = [None] * (width // HEAD)
        for k in range(hist // KEY_STEP):
            for n in range(width // HEAD):
                rows, cols = pl.ds(k * KEY_STEP, KEY_STEP), pl.ds(n * HEAD, HEAD)
                scores = dot_t(queries[:, n * HEAD:(n + 1) * HEAD], key_v[rows, cols])
                scaled = scores * out_scale
                weights = (scaled + scaled * jnp.tanh(scores * arg_scale)).astype(BF)
                term = dot(weights, val_v[rows, cols])
                totals[n] = term if totals[n] is None else totals[n] + term
        mixed = jnp.concatenate(totals, axis=1)
        part(acc, block_a, ch_a)[...] = mixed[:half]
        part(acc, block_b, ch_b)[...] = mixed[half:]

    attend(0, 0, 0, 1)

    def ring(t, _):
        k = lax.div(t + 1, 2)
        ch = lax.rem(t - 1, 2)
        to_right(0, k, ch, t).wait_recv()

        @pl.when(t <= 4)
        def _():
            to_right(k, k + 1, ch, t + 2).start()

        @pl.when(t == 5)
        def _():
            to_right(k, k + 1, ch, 7).start()

        to_left(0, n_ctx - k, ch, t).wait_recv()

        @pl.when(t <= 4)
        def _():
            to_left(n_ctx - k, n_ctx - k - 1, ch, t + 2).start()

        @pl.when(t == 6)
        def _():
            to_left(n_ctx - k, n_ctx - k - 1, ch, 7).start()

        attend(k, ch, n_ctx - k, ch)
        return 0

    lax.fori_loop(1, 7, ring, 0)

    def rs_right(step, ch):
        return send(part(po, step - 1, ch), part(pin_l, step - 1, ch),
                    rs_ss.at[0, step - 1, ch], rs_rs.at[0, step - 1, ch], "ctx", right)

    def rs_left(step, ch):
        return send(part(po, 3 + step, ch), part(pin_r, step - 1, ch),
                    rs_ss.at[1, step - 1, ch], rs_rs.at[1, step - 1, ch], "ctx", left)

    def pass_right(step, ch, add):
        total = part(acc, 3 + step, ch)[...]
        if add:
            rs_right(step - 1, ch).wait_recv()
            total = total + part(pin_l, step - 2, ch)[...].astype(F32)
        part(po, step - 1, ch)[...] = total.astype(BF)
        rs_right(step, ch).start()

    def pass_left(step, ch, add):
        total = part(acc, 5 - step, ch)[...]
        if add:
            rs_left(step - 1, ch).wait_recv()
            total = total + part(pin_r, step - 2, ch)[...].astype(F32)
        part(po, 3 + step, ch)[...] = total.astype(BF)
        rs_left(step, ch).start()

    pass_right(2, 1, False)
    pass_left(2, 0, False)
    to_right(0, 4, 0, 7).wait_recv()
    to_left(0, 4, 1, 7).wait_recv()
    attend(4, 0, 4, 1)
    pass_right(1, 0, False)
    pass_left(1, 1, False)

    arrived(sg, rg, sg_ss, sg_rs)
    gate_v[...] = dot(unhot_v[...], rg[...].reshape(slot_total, width))

    pass_right(3, 1, True)
    pass_left(3, 0, True)
    pass_right(2, 0, True)
    pass_left(2, 1, True)
    pass_right(4, 1, True)
    pass_left(4, 0, True)
    pass_right(3, 0, True)
    pass_left(3, 1, True)
    pass_right(4, 0, True)
    pass_left(4, 1, True)

    def xg_copy(k, ch):
        return send(part(g_all, 0, ch), part(g_all, k, ch), xg_ss.at[k, ch], xg_rs.at[k, ch],
                    "head", lax.rem(h + k, n_head))

    for ch in (0, 1):
        rs_right(4, ch).wait_recv()
        rs_left(4, ch).wait_recv()
        attended = part(acc, 0, ch)[...] + part(pin_l, 3, ch)[...].astype(F32) + part(pin_r, 3, ch)[...].astype(F32)
        rows = slice(ch * half, (ch + 1) * half)
        part(g_all, 0, ch)[...] = (attended * gate_v[rows]).astype(BF)
        for k in (2, 1, 3):
            xg_copy(k, ch).start()

    for k in range(1, n_head):
        wx_copy(k).wait_recv()
    for ch in (0, 1):
        total = dot(part(g_all, 0, ch)[...], wx[0])
        for k in (1, 3, 2):
            xg_copy(k, ch).wait_recv()
            total = total + dot(part(g_all, k, ch)[...], wx[k])
        out_ref[ch * half:(ch + 1) * half] = total.astype(BF)

    drained(req_out, req_in, req_ss, req_rs)
    drained(sq, rq, sq_ss, sq_rs)
    drained(sg, rg, sg_ss, sg_rs)
    for k in range(1, n_head):
        wx_copy(k).wait_send()
        for ch in (0, 1):
            xg_copy(k, ch).wait_send()
    for number in range(1, 8):
        to_right(0, 1, 0, number).wait_send()
        to_left(0, 1, 0, number).wait_send()
    for step in range(1, 5):
        for ch in (0, 1):
            if step > 1 or ch == 0:
                rs_right(step, ch).wait_send()
            if step > 1 or ch == 1:
                rs_left(step, ch).wait_send()


def per_device(catalog, cand_owner, cand_row, hist_len, proj_weight, keys, values, out_weight):
    n_user, n_ctx, n_head = (lax.axis_size(a) for a in ("user", "ctx", "head"))
    cand = cand_row.shape[1]
    rows, model = catalog.shape
    hist, width = keys.shape[1:]
    slots = n_user * SLOTS
    any_space = pl.BlockSpec(memory_space=pl.ANY)
    vmem = pl.BlockSpec(memory_space=pltpu.VMEM)
    dma = pltpu.SemaphoreType.DMA
    piece = (n_user, SLOTS, width)
    ranked = pl.pallas_call(
        functools.partial(kernel, n_user, n_ctx, n_head),
        out_shape=jax.ShapeDtypeStruct((cand, width), BF),
        in_specs=[any_space, vmem, vmem, vmem, any_space, any_space, any_space, any_space],
        out_specs=vmem,
        scratch_shapes=[
            pltpu.VMEM((rows, model), BF),
            pltpu.VMEM((2, model, width), BF),
            pltpu.VMEM((hist, width), BF),
            pltpu.VMEM((hist, width), BF),
            pltpu.VMEM((width, model), BF),
            pltpu.VMEM((n_user, 1, 128), jnp.int32),
            pltpu.VMEM((n_user, 1, 128), jnp.int32),
            pltpu.VMEM((rows, width), BF),
            pltpu.VMEM((rows, width), BF),
            pltpu.VMEM((slots, rows), BF),
            pltpu.VMEM((cand, slots), BF),
            pltpu.VMEM(piece, BF),
            pltpu.VMEM(piece, BF),
            pltpu.VMEM(piece, BF),
            pltpu.VMEM(piece, BF),
            pltpu.VMEM((n_ctx, cand, width), BF),
            pltpu.VMEM((n_ctx, cand, width), F32),
            pltpu.VMEM((8, cand, width), BF),
            pltpu.VMEM((4, cand, width), BF),
            pltpu.VMEM((4, cand, width), BF),
            pltpu.VMEM((cand, width), F32),
            pltpu.VMEM((n_head, cand, width), BF),
            pltpu.VMEM((n_head, width, width), BF),
            dma((5,)),
            dma((n_user,)), dma((n_user,)),
            dma((n_user,)), dma((n_user,)),
            dma((n_user,)), dma((n_user,)),
            dma((2, 8)), dma((2, 8)),
            dma((2, 4, 2)), dma((2, 4, 2)),
            dma((n_head,)), dma((n_head,)),
            dma((n_head, 2)), dma((n_head, 2)),
        ],
        compiler_params=pltpu.CompilerParams(
            collective_id=0, has_side_effects=True, vmem_limit_bytes=40 * 2**20
        ),
        name="rank_items",
    )(
        catalog,
        cand_owner.reshape(1, cand),
        cand_row,
        hist_len.reshape(1, 1),
        jnp.transpose(proj_weight, (1, 0, 2)),
        keys.reshape(hist, width),
        values.reshape(hist, width),
        out_weight,
    )
    return ranked.reshape(1, cand, width)


def solution(mesh):
    return jax.shard_map(
        per_device,
        mesh=mesh,
        in_specs=(
            P("user", None),
            P("user", "ctx", None),
            P("user", "ctx"),
            P("user"),
            P(None, None, "head"),
            P("user", "ctx", "head"),
            P("user", "ctx", "head"),
            P("head", None),
        ),
        out_specs=P("user", "ctx", "head"),
        check_vma=False,
    )
```

time: 172 us -> 74.8 us (0.43)
  the two profiles are of different devices: /device:TPU:8 before, /device:TPU:6 now
where the time goes in v1:
time: 74.8 us; the launch traced here: 74.6 us
  Pallas kernels  68.8 us (92%)
  local copies, waits for them, and re-layouts  5.06 us (7%)
    pallas_call x1, Pallas kernels, per_device(): pl.pallas_call(functools.partial(kernel, n_user, n_ctx, n_head), out_shap...  68.8 us
    unnamed x14, local copies, waits for them, and re-layouts  5.06 us

profile of v1, /device:TPU:6, one launch (start us, length us, event | category | flops | bytes accessed | tf_op | source)
XLA Modules:
  0.0 74.6 jit_solution(2138416818881872488)
XLA Ops:
  0.7 0.0 copy-start
  0.7 0.0 copy-start.1
  0.7 0.0 copy-start.5
  0.7 1.5 %copy.11 = bf16[1024,2,256]{2,0,1:T(8,128)(2,1)S(1)} copy(bf16[1024,2,256]{2,1,0:T(2,128)(2,1)} %param.12) | data formatting | bytes 2097152 | tf_op args[4]
  2.2 0.0 copy-start.4
  2.2 0.0 copy-done
  2.2 0.2 copy-done.1
  2.4 0.0 copy-done.5
  2.4 0.5 copy-done.4
  2.9 0.0 copy-start.2
  2.9 1.1 %copy-done.2 = bf16[1,1536,256]{2,1,0:T(8,128)(2,1)S(1)} copy-done((bf16[1,1536,256]{2,1,0:T(8,128)(2,1)S(1)}, bf16[1,1536,256]{2,1,0:T(8,128)(2,1)}, u32[]{:S(2)}) %copy-start.2) | copy-done | bytes 786456
  4.1 0.0 copy-start.3
  4.1 1.0 %copy-done.3 = bf16[256,1024]{1,0:T(8,128)(2,1)S(1)} copy-done((bf16[256,1024]{1,0:T(8,128)(2,1)S(1)}, bf16[256,1024]{1,0:T(8,128)(2,1)}, u32[]{:S(2)}) %copy-start.3) | copy-done | bytes 524312
  5.1 68.8 %rank_items.1 = bf16[256,256]{1,0:T(8,128)(2,1)S(1)} custom-call(bf16[512,1024]{1,0:T(8,128)(2,1)S(1)} %copy-done, s32[1,256]{1,0:T(1,128)S(1)} %bitcast.13, s32[1,256]{1,0:T(1,128)S(1)} %copy-done.5, s32[1,1]{1,0:T(1,128)} %bitcast.8.len_ref, bf16[2,1024,256]{2,1,0:T(8,128)(2,1)S(1)} %bitcast.9, bf16[1536,256]{1,0:T(8,128)(2,1)S(1)} %bitcast.10, ...), custom_call_target="tpu_custom_call" | custom-call | tf_op jit(solution)/shard_map/rank_items/pallas_call | solution.py:329
  73.9 0.7 copy.14
Async XLA Ops:
  0.7 1.5 %copy-start = (bf16[512,1024]{1,0:T(8,128)(2,1)S(1)}, bf16[512,1024]{1,0:T(8,128)(2,1)}, u32[]{:S(2)}) copy-start(bf16[512,1024]{1,0:T(8,128)(2,1)} %cat_hbm.1) | copy-start | bytes 3145732
  0.7 1.8 %copy-start.1 = (bf16[1,1536,256]{2,1,0:T(8,128)(2,1)S(1)}, bf16[1,1536,256]{2,1,0:T(8,128)(2,1)}, u32[]{:S(2)}) copy-start(bf16[1,1536,256]{2,1,0:T(8,128)(2,1)} %param.13) | copy-start | bytes 2359300
  0.7 1.7 %copy-start.5 = (s32[1,256]{1,0:T(1,128)S(1)}, s32[1,256]{1,0:T(1,128)}, u32[]{:S(2)}) copy-start(s32[1,256]{1,0:T(1,128)} %row_ref.1) | copy-start | bytes 3076
  2.2 0.7 copy-start.4
  2.9 1.1 %copy-start.2 = (bf16[1,1536,256]{2,1,0:T(8,128)(2,1)S(1)}, bf16[1,1536,256]{2,1,0:T(8,128)(2,1)}, u32[]{:S(2)}) copy-start(bf16[1,1536,256]{2,1,0:T(8,128)(2,1)} %param.14) | copy-start | bytes 2359300
  4.1 1.0 %copy-start.3 = (bf16[256,1024]{1,0:T(8,128)(2,1)S(1)}, bf16[256,1024]{1,0:T(8,128)(2,1)}, u32[]{:S(2)}) copy-start(bf16[256,1024]{1,0:T(8,128)(2,1)} %wout_hbm.1) | copy-start | bytes 1572868

commit v2 on v1

--- a/solution.py
+++ b/solution.py
@@ -12,7 +12,8 @@
 BF = jnp.bfloat16
 F32 = jnp.float32
 SLOTS = 32
-KEY_STEP = 512
+KEY_STEP = 768
+CHUNKS = 4
 
 
 def send(src, dst, ssem, rsem, axis, index):
@@ -43,7 +44,7 @@
     n_user, n_ctx, n_head,
     cat_hbm, owner_ref, row_ref, len_ref, w_hbm, key_hbm, val_hbm, wout_hbm,
     out_ref,
-    cat_v, w_v, key_v, val_v, wout_v,
+    cat_v, w_pairs, w_v, key_v, val_v, wout_v,
     req_out, req_in, tab_q, tab_g, hot_v, unhot_v, sq, sg, rq, rg,
     q_all, acc, po, pin_l, pin_r, gate_v, g_all, wx,
     load_sem, req_ss, req_rs, sq_ss, sq_rs, sg_ss, sg_rs,
@@ -55,18 +56,11 @@
     right, left = lax.rem(c + 1, n_ctx), lax.rem(c + n_ctx - 1, n_ctx)
     cand = owner_ref.shape[1]
     half = cand // 2
+    chunk = cand // CHUNKS
     hist = key_v.shape[0]
     width = key_v.shape[1]
+    model = cat_v.shape[1]
     slot_total = n_user * SLOTS
-
-    loads = [
-        pltpu.make_async_copy(a, b, load_sem.at[i])
-        for i, (a, b) in enumerate(
-            ((cat_hbm, cat_v), (w_hbm, w_v), (wout_hbm, wout_v), (key_hbm, key_v), (val_hbm, val_v))
-        )
-    ]
-    for copy in loads:
-        copy.start()
 
     barrier = pltpu.get_barrier_semaphore()
 
@@ -79,6 +73,15 @@
         pl.semaphore_signal(barrier, inc=1, device_id={"ctx": other}, device_id_type=MESH)
     for k in range(1, n_head):
         pl.semaphore_signal(barrier, inc=1, device_id={"head": lax.rem(h + k, n_head)}, device_id_type=MESH)
+
+    loads = [
+        pltpu.make_async_copy(a, b, load_sem.at[i])
+        for i, (a, b) in enumerate(
+            ((cat_hbm, cat_v), (w_hbm, w_pairs), (wout_hbm, wout_v), (key_hbm, key_v), (val_hbm, val_v))
+        )
+    ]
+    for copy in loads:
+        copy.start()
 
     owner = owner_ref[...].astype(F32)
     owner_col = column(owner, cand)
@@ -133,6 +136,14 @@
 
     loads[0].wait()
     loads[1].wait()
+    to = lax.broadcasted_iota(jnp.int32, (256, 256), 0)
+    source = jnp.where(to < 128, 2 * to, 2 * to - 255)
+    split = jnp.where(source == lax.broadcasted_iota(jnp.int32, (256, 256), 1), 1.0, 0.0).astype(BF)
+    pairs = w_pairs[...].reshape(2 * model, width)
+    for i in range(model // 128):
+        apart = dot(split, pairs[256 * i:256 * (i + 1)]).astype(BF)
+        w_v[0, 128 * i:128 * (i + 1)] = apart[:128]
+        w_v[1, 128 * i:128 * (i + 1)] = apart[128:]
     tab_q[...] = silu(dot(cat_v[...], w_v[0])).astype(BF)
     tab_g[...] = silu(dot(cat_v[...], w_v[1])).astype(BF)
 
@@ -147,6 +158,7 @@
         wx_copy(k).start()
     wx[0] = wout_v[:, pl.ds(pl.multiple_of(h * width, width), width)]
 
+    acc[...] = jnp.zeros_like(acc)
     arrived(req_out, req_in, req_ss, req_rs)
     row_lane = lax.broadcasted_iota(jnp.int32, (128, cat_v.shape[0]), 1).astype(F32)
     for g in range(n_user // 4):
@@ -155,23 +167,24 @@
         hot_v[128 * g:128 * (g + 1)] = hot.astype(BF)
     sq[...] = dot(hot_v[...], tab_q[...]).astype(BF).reshape(sq.shape)
     exchange(sq, rq, sq_ss, sq_rs)
-    sg[...] = dot(hot_v[...], tab_g[...]).astype(BF).reshape(sg.shape)
-    exchange(sg, rg, sg_ss, sg_rs)
 
     loads[3].wait()
     loads[4].wait()
-    length = len_ref[...]
+    length = len_ref[0]
     place = lax.broadcasted_iota(jnp.int32, (hist, width), 0) + c * hist
     val_v[...] = jnp.where(place < length, val_v[...].astype(F32), 0.0).astype(BF)
     scale = HEAD ** -0.5
     arg_scale = 0.5 * scale
-    out_scale = jnp.broadcast_to((0.5 * scale) / length.astype(F32), (1, KEY_STEP))
+    out_scale = (0.5 * scale) / jnp.full((1, KEY_STEP), length, jnp.int32).astype(F32)
 
     arrived(sq, rq, sq_ss, sq_rs)
     q_all[0] = dot(unhot_v[...], rq[...].reshape(slot_total, width)).astype(BF)
 
     def part(ref, block, ch):
-        return ref.at[block, pl.ds(pl.multiple_of(ch * half, half), half)]
+        return ref.at[block, pl.ds(pl.multiple_of(ch * chunk, chunk), chunk)]
+
+    def half_of(ref, block, j):
+        return ref.at[block, pl.ds(pl.multiple_of(j * half, half), half)]
 
     def to_right(src_block, dst_block, ch, number):
         return send(part(q_all, src_block, ch), part(q_all, dst_block, ch),
@@ -181,54 +194,23 @@
         return send(part(q_all, src_block, ch), part(q_all, dst_block, ch),
                     ag_ss.at[1, number], ag_rs.at[1, number], "ctx", left)
 
-    for ch in (0, 1):
-        to_right(0, 1, ch, ch + 1).start()
-        to_left(0, n_ctx - 1, ch, ch + 1).start()
-
-    def attend(block_a, ch_a, block_b, ch_b):
-        queries = jnp.concatenate([part(q_all, block_a, ch_a)[...], part(q_all, block_b, ch_b)[...]], axis=0)
-        totals = [None] * (width // HEAD)
-        for k in range(hist // KEY_STEP):
-            for n in range(width // HEAD):
-                rows, cols = pl.ds(k * KEY_STEP, KEY_STEP), pl.ds(n * HEAD, HEAD)
-                scores = dot_t(queries[:, n * HEAD:(n + 1) * HEAD], key_v[rows, cols])
-                scaled = scores * out_scale
-                weights = (scaled + scaled * jnp.tanh(scores * arg_scale)).astype(BF)
-                term = dot(weights, val_v[rows, cols])
-                totals[n] = term if totals[n] is None else totals[n] + term
-        mixed = jnp.concatenate(totals, axis=1)
-        part(acc, block_a, ch_a)[...] = mixed[:half]
-        part(acc, block_b, ch_b)[...] = mixed[half:]
-
-    attend(0, 0, 0, 1)
-
-    def ring(t, _):
-        k = lax.div(t + 1, 2)
-        ch = lax.rem(t - 1, 2)
-        to_right(0, k, ch, t).wait_recv()
-
-        @pl.when(t <= 4)
-        def _():
-            to_right(k, k + 1, ch, t + 2).start()
-
-        @pl.when(t == 5)
-        def _():
-            to_right(k, k + 1, ch, 7).start()
-
-        to_left(0, n_ctx - k, ch, t).wait_recv()
-
-        @pl.when(t <= 4)
-        def _():
-            to_left(n_ctx - k, n_ctx - k - 1, ch, t + 2).start()
-
-        @pl.when(t == 6)
-        def _():
-            to_left(n_ctx - k, n_ctx - k - 1, ch, 7).start()
-
-        attend(k, ch, n_ctx - k, ch)
-        return 0
-
-    lax.fori_loop(1, 7, ring, 0)
+    for i in range(CHUNKS):
+        to_right(0, 1, i, i).start()
+        to_left(0, n_ctx - 1, CHUNKS - 1 - i, i).start()
+
+    def attend(block_a, half_a, block_b, half_b, piece):
+        queries = jnp.concatenate([half_of(q_all, block_a, half_a)[...], half_of(q_all, block_b, half_b)[...]], axis=0)
+        rows = pl.ds(pl.multiple_of(piece * KEY_STEP, KEY_STEP), KEY_STEP)
+        terms = []
+        for n in range(width // HEAD):
+            cols = pl.ds(n * HEAD, HEAD)
+            scores = dot_t(queries[:, n * HEAD:(n + 1) * HEAD], key_v[rows, cols])
+            scaled = scores * out_scale
+            weights = (scaled + scaled * jnp.tanh(scores * arg_scale)).astype(BF)
+            terms.append(dot(weights, val_v[rows, cols]))
+        mixed = jnp.concatenate(terms, axis=1)
+        half_of(acc, block_a, half_a)[...] += mixed[:half]
+        half_of(acc, block_b, half_b)[...] += mixed[half:]
 
     def rs_right(step, ch):
         return send(part(po, step - 1, ch), part(pin_l, step - 1, ch),
@@ -254,66 +236,104 @@
         part(po, 3 + step, ch)[...] = total.astype(BF)
         rs_left(step, ch).start()
 
-    pass_right(2, 1, False)
-    pass_left(2, 0, False)
-    to_right(0, 4, 0, 7).wait_recv()
-    to_left(0, 4, 1, 7).wait_recv()
-    attend(4, 0, 4, 1)
-    pass_right(1, 0, False)
-    pass_left(1, 1, False)
+    far = [(i, CHUNKS - 1 - i) for i in range(CHUNKS // 2)]
+    near = [(CHUNKS // 2 + i, CHUNKS // 2 - 1 - i) for i in range(CHUNKS // 2)]
+
+    def pass_on(step, pairs, add):
+        for r, l in pairs:
+            pass_right(step, r, add)
+            pass_left(step, l, add)
+
+    sg[...] = dot(hot_v[...], tab_g[...]).astype(BF).reshape(sg.shape)
+    exchange(sg, rg, sg_ss, sg_rs)
+    pieces = hist // KEY_STEP
+    for p in range(pieces):
+        attend(0, 0, 0, 1, p)
+
+    last = 3 * CHUNKS + CHUNKS // 2
+    quarter = CHUNKS // 4
+
+    def ring(t, _):
+        k = lax.div(t, CHUNKS) + 1
+        i = lax.rem(t, CHUNKS)
+        to_right(0, k, i, t).wait_recv()
+
+        @pl.when(t < last - CHUNKS)
+        def _():
+            to_right(k, k + 1, i, t + CHUNKS).start()
+
+        to_left(0, n_ctx - k, CHUNKS - 1 - i, t).wait_recv()
+
+        @pl.when(t < last - CHUNKS)
+        def _():
+            to_left(n_ctx - k, n_ctx - k - 1, CHUNKS - 1 - i, t + CHUNKS).start()
+
+        due = lax.div(t + 1, quarter) - 2
+        task = lax.div(due, 2)
+
+        @pl.when((lax.rem(t + 1, quarter) == 0) & (due >= 0) & (task < 6))
+        def _():
+            block = lax.div(task, 2) + 1
+            j = lax.rem(task, 2)
+            attend(block, j, n_ctx - block, 1 - j, lax.rem(due, 2))
+
+        @pl.when(t == 11 * quarter - 1)
+        def _():
+            pass_on(2, near, False)
+
+        return 0
+
+    lax.fori_loop(0, last, ring, 0)
+    for p in range(pieces):
+        attend(4, 0, 4, 1, p)
+    pass_on(1, far, False)
 
     arrived(sg, rg, sg_ss, sg_rs)
     gate_v[...] = dot(unhot_v[...], rg[...].reshape(slot_total, width))
 
-    pass_right(3, 1, True)
-    pass_left(3, 0, True)
-    pass_right(2, 0, True)
-    pass_left(2, 1, True)
-    pass_right(4, 1, True)
-    pass_left(4, 0, True)
-    pass_right(3, 0, True)
-    pass_left(3, 1, True)
-    pass_right(4, 0, True)
-    pass_left(4, 1, True)
+    pass_on(3, near, True)
+    pass_on(2, far, True)
+    pass_on(4, near, True)
+    pass_on(3, far, True)
+    pass_on(4, far, True)
 
     def xg_copy(k, ch):
         return send(part(g_all, 0, ch), part(g_all, k, ch), xg_ss.at[k, ch], xg_rs.at[k, ch],
                     "head", lax.rem(h + k, n_head))
 
-    for ch in (0, 1):
+    order = [ch for pair in far for ch in pair]
+    for ch in order:
         rs_right(4, ch).wait_recv()
         rs_left(4, ch).wait_recv()
         attended = part(acc, 0, ch)[...] + part(pin_l, 3, ch)[...].astype(F32) + part(pin_r, 3, ch)[...].astype(F32)
-        rows = slice(ch * half, (ch + 1) * half)
+        rows = slice(ch * chunk, (ch + 1) * chunk)
         part(g_all, 0, ch)[...] = (attended * gate_v[rows]).astype(BF)
         for k in (2, 1, 3):
             xg_copy(k, ch).start()
 
     for k in range(1, n_head):
         wx_copy(k).wait_recv()
-    for ch in (0, 1):
+    for ch in order:
         total = dot(part(g_all, 0, ch)[...], wx[0])
         for k in (1, 3, 2):
             xg_copy(k, ch).wait_recv()
             total = total + dot(part(g_all, k, ch)[...], wx[k])
-        out_ref[ch * half:(ch + 1) * half] = total.astype(BF)
+        out_ref[ch * chunk:(ch + 1) * chunk] = total.astype(BF)
 
     drained(req_out, req_in, req_ss, req_rs)
     drained(sq, rq, sq_ss, sq_rs)
     drained(sg, rg, sg_ss, sg_rs)
     for k in range(1, n_head):
         wx_copy(k).wait_send()
-        for ch in (0, 1):
+        for ch in range(CHUNKS):
             xg_copy(k, ch).wait_send()
-    for number in range(1, 8):
+    for number in range(last):
         to_right(0, 1, 0, number).wait_send()
         to_left(0, 1, 0, number).wait_send()
     for step in range(1, 5):
-        for ch in (0, 1):
-            if step > 1 or ch == 0:
-                rs_right(step, ch).wait_send()
-            if step > 1 or ch == 1:
-                rs_left(step, ch).wait_send()
+        for r, l in far if step == 1 else far + near:
+            rs_right(step, r).wait_send()
+            rs_left(step, l).wait_send()
 
 
 def per_device(catalog, cand_owner, cand_row, hist_len, proj_weight, keys, values, out_weight):
@@ -322,17 +342,19 @@
     rows, model = catalog.shape
     hist, width = keys.shape[1:]
     slots = n_user * SLOTS
-    any_space = pl.BlockSpec(memory_space=pl.ANY)
+    any_space = pl.BlockSpec(memory_space=pltpu.HBM)
     vmem = pl.BlockSpec(memory_space=pltpu.VMEM)
+    smem = pl.BlockSpec(memory_space=pltpu.SMEM)
     dma = pltpu.SemaphoreType.DMA
     piece = (n_user, SLOTS, width)
     ranked = pl.pallas_call(
         functools.partial(kernel, n_user, n_ctx, n_head),
         out_shape=jax.ShapeDtypeStruct((cand, width), BF),
-        in_specs=[any_space, vmem, vmem, vmem, any_space, any_space, any_space, any_space],
+        in_specs=[any_space, vmem, vmem, smem, any_space, any_space, any_space, any_space],
         out_specs=vmem,
         scratch_shapes=[
             pltpu.VMEM((rows, model), BF),
+            pltpu.VMEM((model, 2, width), BF),
             pltpu.VMEM((2, model, width), BF),
             pltpu.VMEM((hist, width), BF),
             pltpu.VMEM((hist, width), BF),
@@ -359,21 +381,21 @@
             dma((n_user,)), dma((n_user,)),
             dma((n_user,)), dma((n_user,)),
             dma((n_user,)), dma((n_user,)),
-            dma((2, 8)), dma((2, 8)),
-            dma((2, 4, 2)), dma((2, 4, 2)),
+            dma((2, 4 * CHUNKS)), dma((2, 4 * CHUNKS)),
+            dma((2, 4, CHUNKS)), dma((2, 4, CHUNKS)),
             dma((n_head,)), dma((n_head,)),
-            dma((n_head, 2)), dma((n_head, 2)),
+            dma((n_head, CHUNKS)), dma((n_head, CHUNKS)),
         ],
         compiler_params=pltpu.CompilerParams(
-            collective_id=0, has_side_effects=True, vmem_limit_bytes=40 * 2**20
+            collective_id=0, has_side_effects=True, vmem_limit_bytes=60 * 2**20
         ),
         name="rank_items",
     )(
         catalog,
         cand_owner.reshape(1, cand),
         cand_row,
-        hist_len.reshape(1, 1),
-        jnp.transpose(proj_weight, (1, 0, 2)),
+        hist_len,
+        proj_weight,
         keys.reshape(hist, width),
         values.reshape(hist, width),
         out_weight,

time: 74.8 us -> 68.5 us (0.916)
  the two profiles are of different devices: /device:TPU:6 before, /device:TPU:8 now
where the time goes in v2:
time: 68.5 us; the launch traced here: 68.4 us
  Pallas kernels  66.1 us (96%)
  local copies, waits for them, and re-layouts  1.57 us (2%)
    pallas_call x1, Pallas kernels, per_device(): pl.pallas_call(functools.partial(kernel, n_user, n_ctx, n_head), out_shap...  66.1 us
    unnamed x1, local copies, waits for them, and re-layouts  1.57 us

profile of v2, /device:TPU:8, one launch (start us, length us, event | category | flops | bytes accessed | tf_op | source)
XLA Modules:
  0.0 68.4 jit_solution(14337657034141271386)
XLA Ops:
  0.7 66.1 %rank_items.1 = bf16[256,256]{1,0:T(8,128)(2,1)} custom-call(bf16[512,1024]{1,0:T(8,128)(2,1)} %cat_hbm.1, s32[1,256]{1,0:T(1,128)} %bitcast.7, s32[1,256]{1,0:T(1,128)} %row_ref.1, s32[1]{0:T(128)S(6)} %copy.10.len_ref, bf16[1024,2,256]{2,1,0:T(2,128)(2,1)} %w_hbm.1, bf16[1536,256]{1,0:T(8,128)(2,1)} %bitcast.4, bf16[1536,256]{1,0:T(8,128)(2,1)} %bitcast.5, ...), custom_call_target="tpu_custom_call" | custom-call | tf_op jit(solution)/shard_map/rank_items/pallas_call | solution.py:350
  66.8 1.6 %copy.11 = bf16[1,256,256]{2,1,0:T(8,128)(2,1)} copy(bf16[1,256,256]{2,1,0:T(8,128)(2,1)} %bitcast.6) | data formatting | bytes 262144

commit v3 on v2

--- a/solution.py
+++ b/solution.py
@@ -46,14 +46,16 @@
     out_ref,
     cat_v, w_pairs, w_v, key_v, val_v, wout_v,
     req_out, req_in, tab_q, tab_g, hot_v, unhot_v, sq, sg, rq, rg,
+    ids_f, req_f, hot_f, unhot_f, sf, rf,
     q_all, acc, po, pin_l, pin_r, gate_v, g_all, wx,
-    load_sem, req_ss, req_rs, sq_ss, sq_rs, sg_ss, sg_rs,
+    load_sem, req_ss, req_rs, sq_ss, sq_rs, sf_ss, sf_rs, opp_ss, opp_rs, sg_ss, sg_rs,
     ag_ss, ag_rs, rs_ss, rs_rs, wx_ss, wx_rs, xg_ss, xg_rs,
 ):
     u = lax.axis_index("user")
     c = lax.axis_index("ctx")
     h = lax.axis_index("head")
     right, left = lax.rem(c + 1, n_ctx), lax.rem(c + n_ctx - 1, n_ctx)
+    opposite = lax.rem(c + n_ctx // 2, n_ctx)
     cand = owner_ref.shape[1]
     half = cand // 2
     chunk = cand // CHUNKS
@@ -69,7 +71,7 @@
         return 0
 
     lax.fori_loop(1, n_user, greet, 0)
-    for other in (left, right):
+    for other in (left, right, opposite):
         pl.semaphore_signal(barrier, inc=1, device_id={"ctx": other}, device_id_type=MESH)
     for k in range(1, n_head):
         pl.semaphore_signal(barrier, inc=1, device_id={"head": lax.rem(h + k, n_head)}, device_id_type=MESH)
@@ -83,15 +85,19 @@
     for copy in loads:
         copy.start()
 
-    owner = owner_ref[...].astype(F32)
-    owner_col = column(owner, cand)
-    first = lax.broadcasted_iota(jnp.int32, (cand, cand), 0)
-    second = lax.broadcasted_iota(jnp.int32, (cand, cand), 1)
-    before = jnp.where((owner_col == owner) & (first < second), 1.0, 0.0)
-    rank = jnp.sum(before, axis=0, keepdims=True)
-    place_col = column(owner * SLOTS + rank, slot_total)
     slot_lane = lax.broadcasted_iota(jnp.int32, (cand, slot_total), 1).astype(F32)
-    unhot_v[...] = jnp.where(place_col == slot_lane, 1.0, 0.0).astype(BF)
+
+    def places(ids):
+        owner = ids.astype(F32)
+        owner_col = column(owner, cand)
+        first = lax.broadcasted_iota(jnp.int32, (cand, cand), 0)
+        second = lax.broadcasted_iota(jnp.int32, (cand, cand), 1)
+        before = jnp.where((owner_col == owner) & (first < second), 1.0, 0.0)
+        rank = jnp.sum(before, axis=0, keepdims=True)
+        place_col = column(owner * SLOTS + rank, slot_total)
+        return owner_col, place_col, jnp.where(place_col == slot_lane, 1.0, 0.0).astype(BF)
+
+    owner_col, place_col, unhot_v[...] = places(owner_ref[...])
     rank_col = place_col[:, :128] - owner_col[:, :128] * SLOTS
     shift = (lax.rem(u, 4) * SLOTS).astype(F32)
     rank_hot = jnp.where(rank_col + shift == slot_lane[:, :128], 1.0, 0.0).astype(BF)
@@ -105,7 +111,7 @@
     for s in range(n_user):
         req_out[s] = asked[s:s + 1]
 
-    pl.semaphore_wait(barrier, n_user - 1 + 2 + n_head - 1)
+    pl.semaphore_wait(barrier, n_user - 1 + 3 + n_head - 1)
 
     def exchange(src, dst, ssem, rsem):
         def start(d, _):
@@ -132,7 +138,10 @@
 
         lax.fori_loop(1, n_user, wait, 0)
 
+    ids_copy = send(owner_ref, ids_f, opp_ss.at[0], opp_rs.at[0], "ctx", opposite)
+    req_copy = send(req_in, req_f, opp_ss.at[1], opp_rs.at[1], "ctx", opposite)
     exchange(req_out, req_in, req_ss, req_rs)
+    ids_copy.start()
 
     loads[0].wait()
     loads[1].wait()
@@ -160,13 +169,47 @@
 
     acc[...] = jnp.zeros_like(acc)
     arrived(req_out, req_in, req_ss, req_rs)
+    req_copy.start()
     row_lane = lax.broadcasted_iota(jnp.int32, (128, cat_v.shape[0]), 1).astype(F32)
-    for g in range(n_user // 4):
-        ids = req_in[4 * g] + req_in[4 * g + 1] + req_in[4 * g + 2] + req_in[4 * g + 3]
-        hot = jnp.where(column(ids.astype(F32), cat_v.shape[0]) == row_lane, 1.0, 0.0)
-        hot_v[128 * g:128 * (g + 1)] = hot.astype(BF)
+
+    def pick(requests, hot_ref):
+        for g in range(n_user // 4):
+            ids = requests[4 * g] + requests[4 * g + 1] + requests[4 * g + 2] + requests[4 * g + 3]
+            hot = jnp.where(column(ids.astype(F32), cat_v.shape[0]) == row_lane, 1.0, 0.0)
+            hot_ref[128 * g:128 * (g + 1)] = hot.astype(BF)
+
+    pick(req_in, hot_v)
     sq[...] = dot(hot_v[...], tab_q[...]).astype(BF).reshape(sq.shape)
     exchange(sq, rq, sq_ss, sq_rs)
+
+    req_copy.wait_recv()
+    pick(req_f, hot_f)
+    sf[...] = dot(hot_f[...], tab_q[...]).astype(BF).reshape(sf.shape)
+    exchange(sf, rf, sf_ss, sf_rs)
+
+    arrived(sq, rq, sq_ss, sq_rs)
+    q_all[0] = dot(unhot_v[...], rq[...].reshape(slot_total, width)).astype(BF)
+
+    def part(ref, block, ch):
+        return ref.at[block, pl.ds(pl.multiple_of(ch * chunk, chunk), chunk)]
+
+    def half_of(ref, block, j):
+        return ref.at[block, pl.ds(pl.multiple_of(j * half, half), half)]
+
+    def to_right(src_block, dst_block, ch, number):
+        return send(part(q_all, src_block, ch), part(q_all, dst_block, ch),
+                    ag_ss.at[0, number], ag_rs.at[0, number], "ctx", right)
+
+    def to_left(src_block, dst_block, ch, number):
+        return send(part(q_all, src_block, ch), part(q_all, dst_block, ch),
+                    ag_ss.at[1, number], ag_rs.at[1, number], "ctx", left)
+
+    for i in range(CHUNKS):
+        to_right(0, 1, i, i).start()
+        to_left(0, n_ctx - 1, CHUNKS - 1 - i, i).start()
+
+    ids_copy.wait_recv()
+    unhot_f[...] = places(ids_f[...])[2]
 
     loads[3].wait()
     loads[4].wait()
@@ -176,27 +219,6 @@
     scale = HEAD ** -0.5
     arg_scale = 0.5 * scale
     out_scale = (0.5 * scale) / jnp.full((1, KEY_STEP), length, jnp.int32).astype(F32)
-
-    arrived(sq, rq, sq_ss, sq_rs)
-    q_all[0] = dot(unhot_v[...], rq[...].reshape(slot_total, width)).astype(BF)
-
-    def part(ref, block, ch):
-        return ref.at[block, pl.ds(pl.multiple_of(ch * chunk, chunk), chunk)]
-
-    def half_of(ref, block, j):
-        return ref.at[block, pl.ds(pl.multiple_of(j * half, half), half)]
-
-    def to_right(src_block, dst_block, ch, number):
-        return send(part(q_all, src_block, ch), part(q_all, dst_block, ch),
-                    ag_ss.at[0, number], ag_rs.at[0, number], "ctx", right)
-
-    def to_left(src_block, dst_block, ch, number):
-        return send(part(q_all, src_block, ch), part(q_all, dst_block, ch),
-                    ag_ss.at[1, number], ag_rs.at[1, number], "ctx", left)
-
-    for i in range(CHUNKS):
-        to_right(0, 1, i, i).start()
-        to_left(0, n_ctx - 1, CHUNKS - 1 - i, i).start()
 
     def attend(block_a, half_a, block_b, half_b, piece):
         queries = jnp.concatenate([half_of(q_all, block_a, half_a)[...], half_of(q_all, block_b, half_b)[...]], axis=0)
@@ -244,58 +266,71 @@
             pass_right(step, r, add)
             pass_left(step, l, add)
 
-    sg[...] = dot(hot_v[...], tab_g[...]).astype(BF).reshape(sg.shape)
-    exchange(sg, rg, sg_ss, sg_rs)
     pieces = hist // KEY_STEP
     for p in range(pieces):
         attend(0, 0, 0, 1, p)
 
-    last = 3 * CHUNKS + CHUNKS // 2
-    quarter = CHUNKS // 4
-
-    def ring(t, _):
+    def come(t):
         k = lax.div(t, CHUNKS) + 1
         i = lax.rem(t, CHUNKS)
-        to_right(0, k, i, t).wait_recv()
-
-        @pl.when(t < last - CHUNKS)
-        def _():
-            to_right(k, k + 1, i, t + CHUNKS).start()
-
-        to_left(0, n_ctx - k, CHUNKS - 1 - i, t).wait_recv()
-
-        @pl.when(t < last - CHUNKS)
-        def _():
-            to_left(n_ctx - k, n_ctx - k - 1, CHUNKS - 1 - i, t + CHUNKS).start()
-
+        return k, i, to_right(0, k, i, t), to_left(0, n_ctx - k, CHUNKS - 1 - i, t)
+
+    last = 3 * CHUNKS
+    quarter = CHUNKS // 4
+
+    def ring(t, _):
+        k, i, from_left, from_right = come(t)
+        from_left.wait_recv()
+        to_right(k, k + 1, i, t + CHUNKS).start()
+        from_right.wait_recv()
+        to_left(n_ctx - k, n_ctx - k - 1, CHUNKS - 1 - i, t + CHUNKS).start()
         due = lax.div(t + 1, quarter) - 2
         task = lax.div(due, 2)
 
-        @pl.when((lax.rem(t + 1, quarter) == 0) & (due >= 0) & (task < 6))
+        @pl.when((lax.rem(t + 1, quarter) == 0) & (due >= 0) & (task < 3))
         def _():
             block = lax.div(task, 2) + 1
             j = lax.rem(task, 2)
             attend(block, j, n_ctx - block, 1 - j, lax.rem(due, 2))
 
-        @pl.when(t == 11 * quarter - 1)
-        def _():
-            pass_on(2, near, False)
-
         return 0
 
-    lax.fori_loop(0, last, ring, 0)
-    for p in range(pieces):
-        attend(4, 0, 4, 1, p)
+    lax.fori_loop(0, last - CHUNKS, ring, 0)
+
+    arrived(sf, rf, sf_ss, sf_rs)
+    q_all[4] = dot(unhot_f[...], rf[...].reshape(slot_total, width)).astype(BF)
+
+    def attend_piece(block_a, half_a, block_b, half_b):
+        def body(p, _):
+            attend(block_a, half_a, block_b, half_b, p)
+            return 0
+
+        lax.fori_loop(0, pieces, body, 0)
+
+    attend_piece(4, 0, 4, 1)
     pass_on(1, far, False)
-
+    sg[...] = dot(hot_v[...], tab_g[...]).astype(BF).reshape(sg.shape)
+    exchange(sg, rg, sg_ss, sg_rs)
+
+    def land(t, _):
+        k, i, from_left, from_right = come(t)
+        from_left.wait_recv()
+        from_right.wait_recv()
+        return 0
+
+    lax.fori_loop(last - CHUNKS, last - CHUNKS // 2, land, 0)
+    attend_piece(3, 0, 5, 1)
+    pass_on(2, near, False)
+    lax.fori_loop(last - CHUNKS // 2, last, land, 0)
+    attend_piece(3, 1, 5, 0)
+    pass_on(2, far, True)
+    attend_piece(2, 1, 6, 0)
+    pass_on(3, near, True)
+    pass_on(3, far, True)
+    pass_on(4, near, True)
+    pass_on(4, far, True)
     arrived(sg, rg, sg_ss, sg_rs)
     gate_v[...] = dot(unhot_v[...], rg[...].reshape(slot_total, width))
-
-    pass_on(3, near, True)
-    pass_on(2, far, True)
-    pass_on(4, near, True)
-    pass_on(3, far, True)
-    pass_on(4, far, True)
 
     def xg_copy(k, ch):
         return send(part(g_all, 0, ch), part(g_all, k, ch), xg_ss.at[k, ch], xg_rs.at[k, ch],
@@ -322,6 +357,9 @@
 
     drained(req_out, req_in, req_ss, req_rs)
     drained(sq, rq, sq_ss, sq_rs)
+    drained(sf, rf, sf_ss, sf_rs)
+    ids_copy.wait_send()
+    req_copy.wait_send()
     drained(sg, rg, sg_ss, sg_rs)
     for k in range(1, n_head):
         wx_copy(k).wait_send()
@@ -369,6 +407,12 @@
             pltpu.VMEM(piece, BF),
             pltpu.VMEM(piece, BF),
             pltpu.VMEM(piece, BF),
+            pltpu.VMEM((1, cand), jnp.int32),
+            pltpu.VMEM((n_user, 1, 128), jnp.int32),
+            pltpu.VMEM((slots, rows), BF),
+            pltpu.VMEM((cand, slots), BF),
+            pltpu.VMEM(piece, BF),
+            pltpu.VMEM(piece, BF),
             pltpu.VMEM((n_ctx, cand, width), BF),
             pltpu.VMEM((n_ctx, cand, width), F32),
             pltpu.VMEM((8, cand, width), BF),
@@ -381,7 +425,9 @@
             dma((n_user,)), dma((n_user,)),
             dma((n_user,)), dma((n_user,)),
             dma((n_user,)), dma((n_user,)),
-            dma((2, 4 * CHUNKS)), dma((2, 4 * CHUNKS)),
+            dma((2,)), dma((2,)),
+            dma((n_user,)), dma((n_user,)),
+            dma((2, 3 * CHUNKS)), dma((2, 3 * CHUNKS)),
             dma((2, 4, CHUNKS)), dma((2, 4, CHUNKS)),
             dma((n_head,)), dma((n_head,)),
             dma((n_head, CHUNKS)), dma((n_head, CHUNKS)),

time: 68.5 us -> 65.7 us (0.959)
  the two profiles are of different devices: /device:TPU:8 before, /device:TPU:64 now
where the time goes in v3:
time: 65.7 us; the launch traced here: 65.6 us
  Pallas kernels  63.4 us (96%)
  local copies, waits for them, and re-layouts  1.57 us (2%)
  between operations  0.66 us (1%)
    pallas_call x1, Pallas kernels, per_device(): pl.pallas_call(functools.partial(kernel, n_user, n_ctx, n_head), out_shap...  63.4 us
    unnamed x1, local copies, waits for them, and re-layouts  1.57 us

profile of v3, /device:TPU:64, one launch (start us, length us, event | category | flops | bytes accessed | tf_op | source)
XLA Modules:
  0.0 65.6 jit_solution(7808071926791319606)
XLA Ops:
  0.7 63.4 %rank_items.1 = bf16[256,256]{1,0:T(8,128)(2,1)} custom-call(bf16[512,1024]{1,0:T(8,128)(2,1)} %cat_hbm.1, s32[1,256]{1,0:T(1,128)} %bitcast.7, s32[1,256]{1,0:T(1,128)} %row_ref.1, s32[1]{0:T(128)S(6)} %copy.10.len_ref, bf16[1024,2,256]{2,1,0:T(2,128)(2,1)} %w_hbm.1, bf16[1536,256]{1,0:T(8,128)(2,1)} %bitcast.4, bf16[1536,256]{1,0:T(8,128)(2,1)} %bitcast.5, ...), custom_call_target="tpu_custom_call" | custom-call | tf_op jit(solution)/shard_map/rank_items/pallas_call | solution.py:388
  64.0 1.6 %copy.11 = bf16[1,256,256]{2,1,0:T(8,128)(2,1)} copy(bf16[1,256,256]{2,1,0:T(8,128)(2,1)} %bitcast.6) | data formatting | bytes 262144

commit v4 on v3

--- a/solution.py
+++ b/solution.py
@@ -42,9 +42,9 @@
 
 def kernel(
     n_user, n_ctx, n_head,
-    cat_hbm, owner_ref, row_ref, len_ref, w_hbm, key_hbm, val_hbm, wout_hbm,
+    cat_hbm, owner_hbm, row_hbm, len_hbm, w_hbm, key_hbm, val_hbm, wout_hbm,
     out_ref,
-    cat_v, w_pairs, w_v, key_v, val_v, wout_v,
+    owner_ref, row_ref, len_ref, cat_v, w_pairs, w_v, key_v, val_v, wout_v,
     req_out, req_in, tab_q, tab_g, hot_v, unhot_v, sq, sg, rq, rg,
     ids_f, req_f, hot_f, unhot_f, sf, rf,
     q_all, acc, po, pin_l, pin_r, gate_v, g_all, wx,
@@ -79,11 +79,14 @@
     loads = [
         pltpu.make_async_copy(a, b, load_sem.at[i])
         for i, (a, b) in enumerate(
-            ((cat_hbm, cat_v), (w_hbm, w_pairs), (wout_hbm, wout_v), (key_hbm, key_v), (val_hbm, val_v))
+            ((cat_hbm, cat_v), (w_hbm, w_pairs), (wout_hbm, wout_v), (key_hbm, key_v), (val_hbm, val_v),
+             (owner_hbm, owner_ref), (row_hbm, row_ref), (len_hbm, len_ref))
         )
     ]
-    for copy in loads:
+    for copy in loads[5:] + loads[:5]:
         copy.start()
+    loads[5].wait()
+    loads[6].wait()
 
     slot_lane = lax.broadcasted_iota(jnp.int32, (cand, slot_total), 1).astype(F32)
 
@@ -172,20 +175,29 @@
     req_copy.start()
     row_lane = lax.broadcasted_iota(jnp.int32, (128, cat_v.shape[0]), 1).astype(F32)
 
-    def pick(requests, hot_ref):
-        for g in range(n_user // 4):
-            ids = requests[4 * g] + requests[4 * g + 1] + requests[4 * g + 2] + requests[4 * g + 3]
-            hot = jnp.where(column(ids.astype(F32), cat_v.shape[0]) == row_lane, 1.0, 0.0)
-            hot_ref[128 * g:128 * (g + 1)] = hot.astype(BF)
-
-    pick(req_in, hot_v)
-    sq[...] = dot(hot_v[...], tab_q[...]).astype(BF).reshape(sq.shape)
-    exchange(sq, rq, sq_ss, sq_rs)
+    def serve(requests, hot_ref, src, dst, ssem, rsem):
+        def group(g, _):
+            four = lax.rem(lax.div(u, 4) + g, n_user // 4) * 4
+            ids = requests[four] + requests[four + 1] + requests[four + 2] + requests[four + 3]
+            hot = jnp.where(column(ids.astype(F32), cat_v.shape[0]) == row_lane, 1.0, 0.0).astype(BF)
+            hot_ref[pl.ds(pl.multiple_of(four * SLOTS, 128), 128)] = hot
+            src[pl.ds(four, 4)] = dot(hot, tab_q[...]).astype(BF).reshape(4, SLOTS, width)
+            for i in range(4):
+                d = lax.rem(four + i - u + n_user, n_user)
+
+                @pl.when(d > 0)
+                def _():
+                    send(src.at[four + i], dst.at[u], ssem.at[d], rsem.at[d], "user", four + i).start()
+
+            return 0
+
+        lax.fori_loop(1, n_user // 4 + 1, group, 0)
+        dst[u] = src[u]
+
+    serve(req_in, hot_v, sq, rq, sq_ss, sq_rs)
 
     req_copy.wait_recv()
-    pick(req_f, hot_f)
-    sf[...] = dot(hot_f[...], tab_q[...]).astype(BF).reshape(sf.shape)
-    exchange(sf, rf, sf_ss, sf_rs)
+    serve(req_f, hot_f, sf, rf, sf_ss, sf_rs)
 
     arrived(sq, rq, sq_ss, sq_rs)
     q_all[0] = dot(unhot_v[...], rq[...].reshape(slot_total, width)).astype(BF)
@@ -213,6 +225,7 @@
 
     loads[3].wait()
     loads[4].wait()
+    loads[7].wait()
     length = len_ref[0]
     place = lax.broadcasted_iota(jnp.int32, (hist, width), 0) + c * hist
     val_v[...] = jnp.where(place < length, val_v[...].astype(F32), 0.0).astype(BF)
@@ -276,7 +289,6 @@
         return k, i, to_right(0, k, i, t), to_left(0, n_ctx - k, CHUNKS - 1 - i, t)
 
     last = 3 * CHUNKS
-    quarter = CHUNKS // 4
 
     def ring(t, _):
         k, i, from_left, from_right = come(t)
@@ -284,14 +296,10 @@
         to_right(k, k + 1, i, t + CHUNKS).start()
         from_right.wait_recv()
         to_left(n_ctx - k, n_ctx - k - 1, CHUNKS - 1 - i, t + CHUNKS).start()
-        due = lax.div(t + 1, quarter) - 2
-        task = lax.div(due, 2)
-
-        @pl.when((lax.rem(t + 1, quarter) == 0) & (due >= 0) & (task < 3))
+
+        @pl.when(lax.rem(t, CHUNKS) == CHUNKS - 1)
         def _():
-            block = lax.div(task, 2) + 1
-            j = lax.rem(task, 2)
-            attend(block, j, n_ctx - block, 1 - j, lax.rem(due, 2))
+            attend(1, 0, n_ctx - 1, 1, k - 1)
 
         return 0
 
@@ -324,9 +332,11 @@
     lax.fori_loop(last - CHUNKS // 2, last, land, 0)
     attend_piece(3, 1, 5, 0)
     pass_on(2, far, True)
+    attend_piece(2, 0, 6, 1)
+    pass_on(3, near, True)
     attend_piece(2, 1, 6, 0)
-    pass_on(3, near, True)
     pass_on(3, far, True)
+    attend_piece(1, 1, 7, 0)
     pass_on(4, near, True)
     pass_on(4, far, True)
     arrived(sg, rg, sg_ss, sg_rs)
@@ -382,15 +392,17 @@
     slots = n_user * SLOTS
     any_space = pl.BlockSpec(memory_space=pltpu.HBM)
     vmem = pl.BlockSpec(memory_space=pltpu.VMEM)
-    smem = pl.BlockSpec(memory_space=pltpu.SMEM)
     dma = pltpu.SemaphoreType.DMA
     piece = (n_user, SLOTS, width)
     ranked = pl.pallas_call(
         functools.partial(kernel, n_user, n_ctx, n_head),
         out_shape=jax.ShapeDtypeStruct((cand, width), BF),
-        in_specs=[any_space, vmem, vmem, smem, any_space, any_space, any_space, any_space],
+        in_specs=[any_space] * 8,
         out_specs=vmem,
         scratch_shapes=[
+            pltpu.VMEM((1, cand), jnp.int32),
+            pltpu.VMEM((1, cand), jnp.int32),
+            pltpu.SMEM((1,), jnp.int32),
             pltpu.VMEM((rows, model), BF),
             pltpu.VMEM((model, 2, width), BF),
             pltpu.VMEM((2, model, width), BF),
@@ -421,7 +433,7 @@
             pltpu.VMEM((cand, width), F32),
             pltpu.VMEM((n_head, cand, width), BF),
             pltpu.VMEM((n_head, width, width), BF),
-            dma((5,)),
+            dma((8,)),
             dma((n_user,)), dma((n_user,)),
             dma((n_user,)), dma((n_user,)),
             dma((n_user,)), dma((n_user,)),
@@ -433,7 +445,7 @@
             dma((n_head, CHUNKS)), dma((n_head, CHUNKS)),
         ],
         compiler_params=pltpu.CompilerParams(
-            collective_id=0, has_side_effects=True, vmem_limit_bytes=60 * 2**20
+            collective_id=0, has_side_effects=True, vmem_limit_bytes=55000 * 2**10
         ),
         name="rank_items",
     )(

time: 65.7 us -> 64.8 us (0.986)
  the two profiles are of different devices: /device:TPU:64 before, /device:TPU:8 now
where the time goes in v4:
time: 64.8 us; the launch traced here: 64.6 us
  Pallas kernels  62.6 us (97%)
  local copies, waits for them, and re-layouts  1.34 us (2%)
  between operations  0.68 us (1%)
    pallas_call x1, Pallas kernels, per_device(): pl.pallas_call(functools.partial(kernel, n_user, n_ctx, n_head), out_shap...  62.6 us
    unnamed x5, local copies, waits for them, and re-layouts  1.34 us

profile of v4, /device:TPU:8, one launch (start us, length us, event | category | flops | bytes accessed | tf_op | source)
XLA Modules:
  0.0 64.6 jit_solution(7467805159026662990)
XLA Ops:
  0.7 0.0 copy-start.1
  0.7 0.0 copy-start
  0.7 0.7 %copy-done.1 = s32[1,256]{1,0:T(1,128)S(1)} copy-done((s32[1,256]{1,0:T(1,128)S(1)}, s32[1,256]{1,0:T(1,128)}, u32[]{:S(2)}) %copy-start.1) | copy-done | bytes 1048
  1.3 0.0 copy-done
  1.3 62.6 %rank_items.1 = bf16[256,256]{1,0:T(8,128)(2,1)S(1)} custom-call(bf16[512,1024]{1,0:T(8,128)(2,1)} %cat_hbm.1, s32[1,256]{1,0:T(1,128)S(1)} %bitcast.5, s32[1,256]{1,0:T(1,128)S(1)} %copy-done.1, s32[1]{0:T(128)S(6)} %copy.10.len_hbm, bf16[1024,2,256]{2,1,0:T(2,128)(2,1)} %w_hbm.1, bf16[1536,256]{1,0:T(8,128)(2,1)} %bitcast.6, bf16[1536,256]{1,0:T(8,128)(2,1)} %bitcast.7, ...), custom_call_target="tpu_custom_call" | custom-call | tf_op jit(solution)/shard_map/rank_items/pallas_call | solution.py:397
  64.0 0.7 %copy.11 = bf16[1,256,256]{2,1,0:T(8,128)(2,1)} copy(bf16[1,256,256]{2,1,0:T(8,128)(2,1)S(1)} %bitcast.4) | data formatting | bytes 262144
Async XLA Ops:
  0.7 0.7 %copy-start.1 = (s32[1,256]{1,0:T(1,128)S(1)}, s32[1,256]{1,0:T(1,128)}, u32[]{:S(2)}) copy-start(s32[1,256]{1,0:T(1,128)} %row_hbm.1) | copy-start | bytes 3076
  0.7 0.7 %copy-start = (s32[1,256,1]{1,2,0:T(1,128)S(1)}, s32[1,256,1]{1,2,0:T(1,128)}, u32[]{:S(2)}) copy-start(s32[1,256,1]{1,2,0:T(1,128)} %param.9) | copy-start | bytes 3076

commit v5 on v4

--- a/solution.py
+++ b/solution.py
@@ -199,6 +199,7 @@
     req_copy.wait_recv()
     serve(req_f, hot_f, sf, rf, sf_ss, sf_rs)
 
+    sg[...] = dot(hot_v[...], tab_g[...]).astype(BF).reshape(sg.shape)
     arrived(sq, rq, sq_ss, sq_rs)
     q_all[0] = dot(unhot_v[...], rq[...].reshape(slot_total, width)).astype(BF)
 
@@ -317,7 +318,6 @@
 
     attend_piece(4, 0, 4, 1)
     pass_on(1, far, False)
-    sg[...] = dot(hot_v[...], tab_g[...]).astype(BF).reshape(sg.shape)
     exchange(sg, rg, sg_ss, sg_rs)
 
     def land(t, _):

time: 64.8 us -> 64.3 us (level)
  no operation moved by 1% of the time
where the time goes in v5:
time: 64.3 us; the launch traced here: 64.2 us
  Pallas kernels  62.2 us (97%)
  local copies, waits for them, and re-layouts  1.34 us (2%)
  between operations  0.68 us (1%)
    pallas_call x1, Pallas kernels, per_device(): pl.pallas_call(functools.partial(kernel, n_user, n_ctx, n_head), out_shap...  62.2 us
    unnamed x5, local copies, waits for them, and re-layouts  1.34 us

profile of v5, /device:TPU:8, one launch (start us, length us, event | category | flops | bytes accessed | tf_op | source)
XLA Modules:
  0.0 64.2 jit_solution(10718659622051503315)
XLA Ops:
  0.7 0.0 copy-start.1
  0.7 0.0 copy-start
  0.7 0.7 %copy-done.1 = s32[1,256]{1,0:T(1,128)S(1)} copy-done((s32[1,256]{1,0:T(1,128)S(1)}, s32[1,256]{1,0:T(1,128)}, u32[]{:S(2)}) %copy-start.1) | copy-done | bytes 1048
  1.3 0.0 copy-done
  1.3 62.2 %rank_items.1 = bf16[256,256]{1,0:T(8,128)(2,1)S(1)} custom-call(bf16[512,1024]{1,0:T(8,128)(2,1)} %cat_hbm.1, s32[1,256]{1,0:T(1,128)S(1)} %bitcast.5, s32[1,256]{1,0:T(1,128)S(1)} %copy-done.1, s32[1]{0:T(128)S(6)} %copy.10.len_hbm, bf16[1024,2,256]{2,1,0:T(2,128)(2,1)} %w_hbm.1, bf16[1536,256]{1,0:T(8,128)(2,1)} %bitcast.6, bf16[1536,256]{1,0:T(8,128)(2,1)} %bitcast.7, ...), custom_call_target="tpu_custom_call" | custom-call | tf_op jit(solution)/shard_map/rank_items/pallas_call | solution.py:397
  63.5 0.7 %copy.11 = bf16[1,256,256]{2,1,0:T(8,128)(2,1)} copy(bf16[1,256,256]{2,1,0:T(8,128)(2,1)S(1)} %bitcast.4) | data formatting | bytes 262144
Async XLA Ops:
  0.7 0.7 %copy-start.1 = (s32[1,256]{1,0:T(1,128)S(1)}, s32[1,256]{1,0:T(1,128)}, u32[]{:S(2)}) copy-start(s32[1,256]{1,0:T(1,128)} %row_hbm.1) | copy-start | bytes 3076
  0.7 0.7 %copy-start = (s32[1,256,1]{1,2,0:T(1,128)S(1)}, s32[1,256,1]{1,2,0:T(1,128)}, u32[]{:S(2)}) copy-start(s32[1,256,1]{1,2,0:T(1,128)} %param.9) | copy-start | bytes 3076
